TPU v7x, 128 devices: a whole 4x4x4 slice. The times are simulated.
128 devices in a mesh: group: 4 (over y), tensor: 32 (over x, z, core).
Axes of the slice: x: 4, y: 4, z: 4, core: 2. Of those that a mesh axis runs over, the one named last changes fastest.
Arguments:
- requests: bfloat16 [2048, 7168], P(('group', 'tensor')), parts along dimension 0, may hold values from -6 to 6
- counts: int32 [128], P('group'), parts along dimension 0, may hold values from 1 to 16, 256 in all
- gate_weight: bfloat16 [7168, 18432], P(None, 'tensor'), may hold values from -0.0625 to 0.0625
- up_weight: bfloat16 [7168, 18432], P(None, 'tensor'), may hold values from -0.0625 to 0.0625
- down_weight: bfloat16 [18432, 7168], P('tensor'), may hold values from -0.046875 to 0.046875
Outputs:
- finished: bfloat16 [2048, 7168], P(('group', 'tensor')), parts along dimension 0
There are 4 independent parts, one for each index of `group`. A program takes and returns all parts, laid end to end along the dimension named above; an argument that names none is the same for every part. Nothing has to cross between parts.
Inputs may be any that keep to these rules, and one draw needn't show every extreme that they name: Each group's counts add up to 256, and in every group some replica holds exactly 16 requests.
All inputs are finite; a program needn't handle non-finite values.
Results may differ from a plain program's by a relative error of at most 0.0058.
Values may be sent and summed in bfloat16 or wider, within the bound.
A program may use at most 128 MiB of HBM per device.

v0:
```python
import jax
import jax.numpy as jnp
from jax import lax
from jax.sharding import PartitionSpec as P

ROWS = 256


def local(requests, counts, gate_weight, up_weight, down_weight):
    members = lax.axis_size("tensor")
    capacity = requests.shape[0]
    features = requests.shape[1]
    offsets = jnp.cumsum(counts) - counts
    row_ends = offsets + counts
    positions = jnp.arange(ROWS, dtype=jnp.int32)
    member_ids = jnp.arange(members, dtype=jnp.int32)
    owners = jnp.sum((positions[:, None] >= row_ends[None, :]).astype(jnp.int32), axis=1)
    owner_table = owners[:, None] == member_ids[None, :]
    row_starts = jnp.sum(jnp.where(owner_table, offsets[None, :], 0), axis=1)
    gathered = lax.all_gather(requests, "tensor", axis=0, tiled=True)
    source = owners * capacity + positions - row_starts
    packed = jnp.take(gathered, source, axis=0)
    gate_sum = jnp.dot(packed, gate_weight, preferred_element_type=jnp.float32)
    up_sum = jnp.dot(packed, up_weight, preferred_element_type=jnp.float32)
    hidden = (jax.nn.silu(gate_sum) * up_sum).astype(jnp.bfloat16)
    slot_index = jnp.arange(capacity, dtype=jnp.int32)
    partial_value = jnp.dot(hidden, down_weight, preferred_element_type=jnp.float32).astype(
        jnp.bfloat16
    )
    wanted = offsets[:, None] + slot_index[None, :]
    in_use = slot_index[None, :] < counts[:, None]
    taken = jnp.take(partial_value, jnp.clip(wanted, 0, ROWS - 1).reshape(-1), axis=0).reshape(
        members, capacity, features
    )
    outgoing = jnp.where(in_use[:, :, None], taken, jnp.zeros_like(taken)).reshape(
        members * capacity, features
    )
    arrived = lax.all_to_all(outgoing, "tensor", split_axis=0, concat_axis=0, tiled=True)
    summed = jnp.sum(arrived.reshape(members, capacity, features), axis=0, dtype=jnp.float32)
    finished = summed.astype(jnp.bfloat16)
    return finished


def solution(mesh):
    return jax.shard_map(
        local,
        mesh=mesh,
        in_specs=(
            P(("group", "tensor"), None),
            P("group"),
            P(None, "tensor"),
            P(None, "tensor"),
            P("tensor", None),
        ),
        out_specs=P(("group", "tensor"), None),
        check_vma=False,
    )
```

profile of v0, /device:TPU:1, one launch (start us, length us, event | category | flops | bytes accessed | tf_op | source)
XLA Modules:
  0.0 223.3 jit_solution(11860320936768552943)
XLA Ops:
  6.5 0.0 all-gather.2.cloned.1.call-start
  6.5 0.7 all-gather.2.cloned.1.call-update
  7.3 0.7 copy.8
  8.0 0.1 reduce-window.8
  8.1 0.1 reduce.2
  8.2 0.7 sub.17
  8.8 0.1 add_clamp_fusion
  8.9 0.1 min.12
  9.0 0.1 convert_reduce_fusion
  9.1 0.1 select_reduce_fusion
  9.2 0.7 iota_compare_fusion.2
  10.0 54.3 %all-gather.2.cloned.1.call-done = bf16[512,7168]{1,0:T(8,128)(2,1)} async-done(((bf16[16,7168]{1,0:T(8,128)(2,1)}), bf16[512,7168]{1,0:T(8,128)(2,1)}) %all-gather.2.cloned.1.call-update) | async-done | bytes 7340048 | tf_op jit(solution)/shard_map/all_gather | solution.py:20
  64.3 12.1 %gather_fusion = bf16[256,7168]{1,0:T(8,128)(2,1)} fusion(bf16[512,7168]{1,0:T(8,128)(2,1)} %all-gather.2.cloned.1.call-done, s32[1024]{0:T(1024)S(1)} %pad_clamp_fusion.1), kind=kCustom, calls=%fused_computation | custom fusion | bytes 7341056 | tf_op jit(solution)/shard_map/jit(_take)/gather | solution.py:22
  76.4 6.9 %fusion.1 = f32[256,576]{0,1:T(8,128)S(1)} fusion(bf16[7168,576]{0,1:T(8,128)(2,1)} %param.7, bf16[256,7168]{1,0:T(8,128)(2,1)} %gather_fusion, pred[256]{0:T(512)(128)(4,1)S(1)} %compare_and_fusion.1), kind=kOutput, calls=%fused_computation.6 | convolution fusion | flops 2115764224 | bytes 12517632 | tf_op jit(solution)/shard_map/dot_general | solution.py:23
  83.3 18.5 %convolution_convert_fusion = bf16[256,7168]{1,0:T(8,128)(2,1)} fusion(bf16[576,7168]{1,0:T(8,128)(2,1)} %param.9, bf16[7168,576]{0,1:T(8,128)(2,1)} %param.8, bf16[256,7168]{1,0:T(8,128)(2,1)} %gather_fusion, pred[256]{0:T(512)(128)(4,1)S(1)} %compare_and_fusion.1, f32[256,576]{0,1:T(8,128)S(1)} %fusion.1), kind=kOutput, calls=%fused_computation.2 | convolution fusion | flops 4232413184 | bytes 24445184 | tf_op jit(solution)/shard_map/dot_general | solution.py:27
  101.8 16.3 %gather_fusion.1 = bf16[512,7168]{1,0:T(8,128)(2,1)} fusion(bf16[256,7168]{1,0:T(8,128)(2,1)} %convolution_convert_fusion, s32[1024]{0:T(1024)S(1)} %pad_clamp_fusion), kind=kCustom, calls=%fused_computation.1 | custom fusion | bytes 14682112 | tf_op jit(solution)/shard_map/jit(_take)/gather | solution.py:32
  118.1 4.0 %select_select_fusion = bf16[32,16,7168]{2,1,0:T(8,128)(2,1)S(1)} fusion(bf16[32,16,7168]{2,1,0:T(8,128)(2,1)} %bitcast.9, pred[32,16]{1,0:T(8,128)(4,1)S(1)} %get-tuple-element.6, pred[32,16]{1,0:T(8,128)(4,1)S(1)} %get-tuple-element.5), kind=kLoop, calls=%fused_computation.3 | loop fusion | flops 7340032 | bytes 14681088 | tf_op jit(solution)/shard_map/jit(_where)/select_n | solution.py:35
  122.1 89.3 %all_to_all.6 = bf16[32,16,7168]{2,1,0:T(8,128)(2,1)} all-to-all(bf16[32,16,7168]{2,1,0:T(8,128)(2,1)S(1)} %select_select_fusion), channel_id=1, replica_groups=mesh['group'=4,'tensor'=32] {'tensor'}, dimensions={0} | all-to-all | bytes 14680064 | tf_op jit(solution)/shard_map/all_to_all | solution.py:38
  211.4 5.1 %reduce_sum.35 = bf16[16,7168]{1,0:T(8,128)(2,1)} reduce(bf16[32,16,7168]{2,1,0:T(8,128)(2,1)} %all_to_all.6, bf16[]{:T(256)} %constant.43.clone.1), dimensions={0}, to_apply=%region_3.4 | reduce | flops 3555328 | bytes 7569410 | tf_op jit(solution)/shard_map/reduce_sum | solution.py:39
  (6 shorter events, 0.0 us)
Async XLA Ops:
  6.5 57.7 %all-gather.2.cloned.1.call-start = ((), (), s32[]{:S(2)}) async-start(), calls=%async_computation.1 | async-start | bytes 7569408 | tf_op jit(solution)/shard_map/all_gather | solution.py:20
Sparse Core Ops, SparseCore 0:
  9.6 54.6 all-gather.1
where the time goes:
time: 224 us; the launch traced here: 223 us
  blocking collectives  89.3 us (40%)
  waiting for transfers between devices  55 us (25%)
  local copies, waits for them, and re-layouts  29.3 us (13%)
  matrix products  25.3 us (11%)
  between operations  13.4 us (6%)
  other arithmetic  10.9 us (5%)
    all_to_all x1, blocking collectives, local(): lax.all_to_all(outgoing, 'tensor', split_axis=0, concat_axis=0, tiled=True)  89.3 us
    all_gather x1, waiting for transfers between devices, local(): gathered = lax.all_gather(requests, 'tensor', axis=0, tiled=True)  54.3 us
    dot_general x1, matrix products, local(): jnp.dot(hidden, down_weight, preferred_element_type=jnp.float32)  18.5 us
    gather x1, local copies, waits for them, and re-layouts, local(): jnp.take(partial_value, jnp.clip(wanted, 0, ROWS - 1).reshape(-1), axis=0)  16.3 us
    gather x1, local copies, waits for them, and re-layouts, local(): packed = jnp.take(gathered, source, axis=0)  12.1 us
    dot_general x1, matrix products, local(): gate_sum = jnp.dot(packed, gate_weight, preferred_element_type=jnp.float32)  6.87 us
    reduce_sum x1, other arithmetic, local(): jnp.sum(arrived.reshape(members, capacity, features), axis=0, dtype=jnp.f...  5.08 us
  transfers between devices with their start and end apart: 1, of which 1 were waited for; matrix products, arithmetic and copies ran while one was open for 1% of the time, Pallas kernels for 0%

commit v1 on v0

v1 whole, which is shorter than its diff:
```python
import functools

import jax
import jax.numpy as jnp
from jax import lax
from jax.experimental import pallas as pl
from jax.experimental.pallas import tpu as pltpu
from jax.sharding import PartitionSpec as P

SIDE = 4
CHIPS = SIDE * SIDE
DEVICES = 2 * CHIPS
CAP = 16
ROWS = 256
LANES = 128
MESH = pl.DeviceIdType.MESH


def stream_widths(half):
    tile = 256 if half % 256 == 0 and half >= 1024 else 128
    tiles = half // tile
    first = (tiles + 3) // 4
    pair = tiles // 2
    return [first * tile, (pair - first) * tile] * 2


def kernel(
    req, counts, wg_hbm, wu_hbm, wd_hbm, out,
    wg, wu, wd, spread, spread2, pkt, rows_in, inbox, grid, gate, up, hidden,
    pout, pin, chip_sum, big_in, quad_sum, small_in, final, rows_out, pkt_back, inbox_back, offs,
    w_sem, a_send, a_recv, g_send, g_recv, r_send, r_recv, b_send, b_recv,
):
    features = req.shape[1]
    half = features // 2
    hb = half // LANES
    rp = inbox.shape[1]
    widths = stream_widths(half)
    starts = [sum(widths[:s]) for s in range(4)]

    me = lax.axis_index("tensor")
    core = lax.rem(me, 2)
    other = 1 - core
    chip = me // 2
    x = chip // SIDE
    z = lax.rem(chip, SIDE)

    def device(xx, zz, cc):
        return {"tensor": (xx * SIDE + zz) * 2 + cc}

    sibling = device(x, z, other)

    barrier = pltpu.get_barrier_semaphore()

    @pl.loop(1, DEVICES)
    def _(s):
        pl.semaphore_signal(
            barrier, inc=1, device_id={"tensor": lax.rem(me + s, DEVICES)}, device_id_type=MESH
        )

    loads = {}
    for turn, c in enumerate((core, other)):
        for s in range(4):
            rows = pl.ds(pl.multiple_of(c * half + starts[s], LANES), widths[s])
            pair = []
            for n, (src, dst) in enumerate(((wg_hbm, wg), (wu_hbm, wu))):
                copy = pltpu.make_async_copy(src.at[rows], dst.at[rows], w_sem.at[turn * 8 + s * 2 + n])
                copy.start()
                pair.append(copy)
            loads[turn, s] = pair
    wd_load = pltpu.make_async_copy(wd_hbm, wd, w_sem.at[16])
    wd_load.start()

    total = jnp.int32(0)
    ends = []
    for i in range(DEVICES):
        offs[i] = total
        total = total + counts[i]
        ends.append(total)
    my_off = offs[me]
    my_count = counts[me]

    spread[...] = jnp.zeros_like(spread)
    for h in range(2):
        for m in range(hb):
            block = req[:, (h * hb + m) * LANES : (h * hb + m + 1) * LANES]
            spread[pl.ds(h * rp + m, CAP, stride=2 * rp), :] = block.astype(jnp.float32)

    def row_for(p, off):
        return lax.rem(p - off + ROWS, CAP)

    for j in range(CAP):
        for h in range(2):
            at = (2 * j + h) * rp
            rows_in[j, h] = spread[at : at + rp, :].astype(jnp.bfloat16)
    for p in range(CHIPS):
        pkt[p] = rows_in[row_for(p, my_off)]
    inbox[me] = pkt[chip, core]

    pl.semaphore_wait(barrier, DEVICES - 1)

    def dispatch(s):
        t = lax.rem(me + s, DEVICES)
        return pltpu.make_async_remote_copy(
            src_ref=pkt.at[t // 2, lax.rem(t, 2)], dst_ref=inbox.at[me],
            send_sem=a_send.at[s], recv_sem=a_recv.at[me],
            device_id={"tensor": t}, device_id_type=MESH,
        )

    def dispatched(s):
        t = lax.rem(me + s, DEVICES)
        return pltpu.make_async_remote_copy(
            src_ref=pkt.at[0, 0], dst_ref=inbox.at[t],
            send_sem=a_send.at[s], recv_sem=a_recv.at[t],
            device_id={"tensor": t}, device_id_type=MESH,
        )

    @pl.loop(1, DEVICES)
    def _(s):
        dispatch(s).start()

    owners = []
    for k in range(ROWS // CHIPS):
        rank = chip + CHIPS * k
        owner = jnp.int32(0)
        for end in ends[:-1]:
            owner = owner + (end <= rank).astype(jnp.int32)
        owners.append(owner)

    @pl.loop(1, DEVICES)
    def _(s):
        dispatched(s).wait_recv()

    for k in range(ROWS // CHIPS):
        spread2[k * rp : (k + 1) * rp, :] = inbox[owners[k]].astype(jnp.float32)
    for m in range(hb):
        block = spread2[pl.ds(m, CAP, stride=rp), :].astype(jnp.bfloat16)
        grid[core, x, z, :, m * LANES : (m + 1) * LANES] = block

    def cols(s):
        return pl.ds(starts[s], widths[s])

    def block_of(s, small, big):
        xx, zz = (small, big) if s < 2 else (big, small)
        return grid.at[core, xx, zz, :, cols(s)]

    def quad_of(buf, s, big):
        return buf.at[:, big, :, cols(s)] if s < 2 else buf.at[big, :, :, cols(s)]

    positions = [(x, z), (x, z), (z, x), (z, x)]
    forward = [(1 - 2 * (s % 2)) * (1 - 2 * core) for s in range(4)]

    def shift(pos, by):
        return lax.rem(pos + by + 2 * SIDE, SIDE)

    def on_small(s, by):
        small, big = positions[s]
        return device(shift(x, by), z, core) if s < 2 else device(x, shift(z, by), core)

    def on_big(s, by):
        return device(x, shift(z, by), core) if s < 2 else device(shift(x, by), z, core)

    def send(src, dst, sends, recvs, index, target):
        copy = pltpu.make_async_remote_copy(
            src_ref=src, dst_ref=dst, send_sem=sends.at[index], recv_sem=recvs.at[index],
            device_id=target, device_id_type=MESH,
        )
        copy.start()
        return copy

    gather = {}

    def gather_block(s, n, small, target):
        ref = block_of(s, small, positions[s][1])
        gather[s, n] = send(ref, ref, g_send, g_recv, s * 10 + n, target)

    def gather_quad(s, n, big, target):
        ref = quad_of(grid.at[core], s, big)
        gather[s, n] = send(ref, ref, g_send, g_recv, s * 10 + n, target)

    order = (0, 2, 1, 3)
    for s in order:
        small, big = positions[s]
        gather_block(s, 0, small, on_small(s, forward[s]))
        gather_block(s, 1, small, on_small(s, -forward[s]))
    for s in order:
        small, big = positions[s]
        gather[s, 0].wait_recv()
        gather_block(s, 2, shift(small, -forward[s]), on_small(s, forward[s]))
    for s in order:
        small, big = positions[s]
        gather[s, 1].wait_recv()
        gather[s, 2].wait_recv()
        gather_quad(s, 3, big, on_big(s, forward[s]))
        gather_quad(s, 4, big, on_big(s, -forward[s]))
        gather_quad(s, 6, big, sibling)
    for s in order:
        small, big = positions[s]
        gather[s, 3].wait_recv()
        gather_quad(s, 5, shift(big, -forward[s]), on_big(s, forward[s]))
        gather_quad(s, 7, shift(big, -forward[s]), sibling)

    first = [True]

    def contract(c, turn, s):
        for copy in loads[turn, s]:
            copy.wait()
        rows = pl.ds(pl.multiple_of(c * half + starts[s], LANES), widths[s])
        lhs = grid[c, :, :, :, starts[s] : starts[s] + widths[s]].reshape(ROWS, widths[s])
        for acc, weight in ((gate, wg), (up, wu)):
            product = jnp.dot(lhs, weight[rows, :], preferred_element_type=jnp.float32)
            if first[0]:
                acc[...] = product
            else:
                acc[...] += product
        first[0] = False

    for s in order:
        small, big = positions[s]
        gather[s, 4].wait_recv()
        gather_quad(s, 8, shift(big, forward[s]), sibling)
        gather[s, 5].wait_recv()
        gather_quad(s, 9, shift(big, 2), sibling)
        contract(core, 0, s)
    for s in order:
        for n in (6, 7, 8, 9):
            gather[s, n].wait_recv()
        contract(other, 1, s)

    value = gate[...]
    hidden[...] = (value / (1.0 + jnp.exp(-value)) * up[...]).astype(jnp.bfloat16)
    wd_load.wait()

    scatter = {}

    def partial_cols(c, s):
        col = pl.ds(pl.multiple_of(c * half + starts[s], LANES), widths[s])
        product = jnp.dot(hidden[...], wd[:, col], preferred_element_type=jnp.float32)
        return product.reshape(SIDE, SIDE, CAP, widths[s])

    def load_cols(buf, s):
        return buf[..., starts[s] : starts[s] + widths[s]]

    def start_stream(s):
        c = cols(s)
        pout[:, :, :, c] = partial_cols(other, s).astype(jnp.bfloat16)
        scatter[s, 0] = send(
            pout.at[:, :, :, c], pin.at[:, :, :, c], r_send, r_recv, s * 7, sibling
        )
        mine = partial_cols(core, s)
        scatter[s, 0].wait_recv()
        chip_sum[:, :, :, c] = (mine + pin[:, :, :, c].astype(jnp.float32)).astype(jnp.bfloat16)
        small, big = positions[s]
        d = forward[s]
        scatter[s, 1] = send(
            quad_of(chip_sum, s, shift(big, 2)), big_in.at[0, :, :, c],
            r_send, r_recv, s * 7 + 1, on_big(s, d),
        )
        scatter[s, 2] = send(
            quad_of(chip_sum, s, shift(big, -d)), big_in.at[1, :, :, c],
            r_send, r_recv, s * 7 + 2, on_big(s, -d),
        )

    def quad_load(s, big):
        c = cols(s)
        return (chip_sum[:, big, :, c] if s < 2 else chip_sum[big, :, :, c]).astype(jnp.float32)

    def relay_quad(s):
        c = cols(s)
        small, big = positions[s]
        d = forward[s]
        scatter[s, 1].wait_recv()
        big_in[0, :, :, c] = (
            quad_load(s, shift(big, d)) + big_in[0, :, :, c].astype(jnp.float32)
        ).astype(jnp.bfloat16)
        scatter[s, 3] = send(
            big_in.at[0, :, :, c], big_in.at[2, :, :, c],
            r_send, r_recv, s * 7 + 3, on_big(s, d),
        )

    def start_small(s):
        c = cols(s)
        small, big = positions[s]
        d = forward[s]
        scatter[s, 2].wait_recv()
        scatter[s, 3].wait_recv()
        quad_sum[:, :, c] = (
            quad_load(s, big)
            + big_in[1, :, :, c].astype(jnp.float32)
            + big_in[2, :, :, c].astype(jnp.float32)
        ).astype(jnp.bfloat16)
        scatter[s, 4] = send(
            quad_sum.at[shift(small, 2), :, c], small_in.at[0, :, c],
            r_send, r_recv, s * 7 + 4, on_small(s, d),
        )
        scatter[s, 5] = send(
            quad_sum.at[shift(small, -d), :, c], small_in.at[1, :, c],
            r_send, r_recv, s * 7 + 5, on_small(s, -d),
        )

    def relay_small(s):
        c = cols(s)
        small, big = positions[s]
        d = forward[s]
        scatter[s, 4].wait_recv()
        small_in[0, :, c] = (
            quad_sum[shift(small, d), :, c].astype(jnp.float32)
            + small_in[0, :, c].astype(jnp.float32)
        ).astype(jnp.bfloat16)
        scatter[s, 6] = send(
            small_in.at[0, :, c], small_in.at[2, :, c],
            r_send, r_recv, s * 7 + 6, on_small(s, d),
        )

    def finish_stream(s):
        c = cols(s)
        small, big = positions[s]
        scatter[s, 5].wait_recv()
        scatter[s, 6].wait_recv()
        final[:, c] = (
            quad_sum[small, :, c].astype(jnp.float32)
            + small_in[1, :, c].astype(jnp.float32)
            + small_in[2, :, c].astype(jnp.float32)
        )

    stages = (start_stream, relay_quad, start_small, relay_small, finish_stream)
    for t in range(len(order) + len(stages) - 1):
        for n, stage in enumerate(stages):
            if 0 <= t - n < len(order):
                stage(order[t - n])

    for m in range(hb):
        spread2[pl.ds(m, CAP, stride=rp), :] = final[:, m * LANES : (m + 1) * LANES]
    for k in range(ROWS // CHIPS):
        rows_out[k] = spread2[k * rp : (k + 1) * rp, :].astype(jnp.bfloat16)
    for i in range(DEVICES):
        rank = offs[i] + row_for(chip, offs[i])
        pkt_back[i] = rows_out[jnp.minimum(rank // CHIPS, ROWS // CHIPS - 1)]
    inbox_back[me] = pkt_back[me]

    def send_back(s):
        t = lax.rem(me + s, DEVICES)
        return pltpu.make_async_remote_copy(
            src_ref=pkt_back.at[t], dst_ref=inbox_back.at[me],
            send_sem=b_send.at[s], recv_sem=b_recv.at[me],
            device_id={"tensor": t}, device_id_type=MESH,
        )

    def sent_back(s):
        t = lax.rem(me + s, DEVICES)
        return pltpu.make_async_remote_copy(
            src_ref=pkt_back.at[0], dst_ref=inbox_back.at[t],
            send_sem=b_send.at[s], recv_sem=b_recv.at[t],
            device_id={"tensor": t}, device_id_type=MESH,
        )

    @pl.loop(1, DEVICES)
    def _(s):
        send_back(s).start()

    @pl.loop(1, DEVICES)
    def _(s):
        dispatch(s).wait_send()

    for copy in list(gather.values()) + list(scatter.values()):
        copy.wait_send()

    @pl.loop(1, DEVICES)
    def _(s):
        sent_back(s).wait_recv()

    for j in range(CAP):
        p = lax.rem(my_off + j, CHIPS)
        for h in range(2):
            row = inbox_back[2 * p + h].astype(jnp.float32)
            row = jnp.where(j < my_count, row, jnp.zeros_like(row))
            spread[(2 * j + h) * rp : (2 * j + h + 1) * rp, :] = row
    for h in range(2):
        for m in range(hb):
            block = spread[pl.ds(h * rp + m, CAP, stride=2 * rp), :]
            at = (h * hb + m) * LANES
            out[:, at : at + LANES] = block.astype(jnp.bfloat16)

    @pl.loop(1, DEVICES)
    def _(s):
        send_back(s).wait_send()


def local(requests, counts, gate_weight, up_weight, down_weight):
    capacity, features = requests.shape
    ff = gate_weight.shape[1]
    half = features // 2
    rp = -(-(half // LANES) // 16) * 16
    bf16, f32 = jnp.bfloat16, jnp.float32
    dma = pltpu.SemaphoreType.DMA
    return pl.pallas_call(
        kernel,
        out_shape=jax.ShapeDtypeStruct((capacity, features), bf16),
        in_specs=[
            pl.BlockSpec(memory_space=pltpu.VMEM),
            pl.BlockSpec(memory_space=pltpu.SMEM),
            pl.BlockSpec(memory_space=pl.ANY),
            pl.BlockSpec(memory_space=pl.ANY),
            pl.BlockSpec(memory_space=pl.ANY),
        ],
        out_specs=pl.BlockSpec(memory_space=pltpu.VMEM),
        scratch_shapes=[
            pltpu.VMEM((features, ff), bf16),
            pltpu.VMEM((features, ff), bf16),
            pltpu.VMEM((ff, features), bf16),
            pltpu.VMEM((CAP * 2 * rp, LANES), f32),
            pltpu.VMEM((CAP * rp, LANES), f32),
            pltpu.VMEM((CHIPS, 2, rp, LANES), bf16),
            pltpu.VMEM((CAP, 2, rp, LANES), bf16),
            pltpu.VMEM((DEVICES, rp, LANES), bf16),
            pltpu.VMEM((2, SIDE, SIDE, CAP, half), bf16),
            pltpu.VMEM((ROWS, ff), f32),
            pltpu.VMEM((ROWS, ff), f32),
            pltpu.VMEM((ROWS, ff), bf16),
            pltpu.VMEM((SIDE, SIDE, CAP, half), bf16),
            pltpu.VMEM((SIDE, SIDE, CAP, half), bf16),
            pltpu.VMEM((SIDE, SIDE, CAP, half), bf16),
            pltpu.VMEM((3, SIDE, CAP, half), bf16),
            pltpu.VMEM((SIDE, CAP, half), bf16),
            pltpu.VMEM((3, CAP, half), bf16),
            pltpu.VMEM((CAP, half), f32),
            pltpu.VMEM((ROWS // CHIPS, rp, LANES), bf16),
            pltpu.VMEM((DEVICES, rp, LANES), bf16),
            pltpu.VMEM((DEVICES, rp, LANES), bf16),
            pltpu.SMEM((DEVICES,), jnp.int32),
            dma((17,)),
            dma((DEVICES,)),
            dma((DEVICES,)),
            dma((40,)),
            dma((40,)),
            dma((28,)),
            dma((28,)),
            dma((DEVICES,)),
            dma((DEVICES,)),
        ],
        compiler_params=pltpu.CompilerParams(
            collective_id=0, has_side_effects=True, vmem_limit_bytes=58 * 2**20
        ),
        cost_estimate=pl.CostEstimate(
            flops=6 * ROWS * features * ff, bytes_accessed=6 * features * ff, transcendentals=ROWS * ff
        ),
        name="ffn",
    )(requests, counts, gate_weight, up_weight, down_weight)


def solution(mesh):
    return jax.shard_map(
        local,
        mesh=mesh,
        in_specs=(
            P(("group", "tensor"), None),
            P("group"),
            P(None, "tensor"),
            P(None, "tensor"),
            P("tensor", None),
        ),
        out_specs=P(("group", "tensor"), None),
        check_vma=False,
    )
```

time: 224 us -> 102 us (0.46)
  blocking collectives: 89.3 us -> 0 us
  Pallas kernels: 0 us -> 75.1 us
  waiting for transfers between devices: 55 us -> 0 us
  matrix products: 25.3 us -> 0 us
  between operations: 13.4 us -> 0.01 us
  other arithmetic: 10.9 us -> 0 us
  local copies, waits for them, and re-layouts: 29.3 us -> 26.4 us
    all_to_all x1 -> x0, blocking collectives: 89.3 us -> none  [local(): lax.all_to_all(outgoing, 'tensor', split_axis=0, concat_axis=0, tiled=True)]
    pallas_call x0 -> x1, Pallas kernels: none -> 75.1 us  [local(): pl.pallas_call(kernel, out_shape=jax.ShapeDtypeStruct((capacity, features...]
    all_gather x1 -> x0, waiting for transfers between devices: 54.3 us -> none  [local(): gathered = lax.all_gather(requests, 'tensor', axis=0, tiled=True)]
    gather x2 -> x0, local copies, waits for them, and re-layouts: 28.4 us -> none  [the longest x1 16.3 us: local(): jnp.take(partial_value, jnp.clip(wanted, 0, ROWS - 1).reshape(-1), axis=0)]
    unnamed x0 -> x3, local copies, waits for them, and re-layouts: none -> 26.4 us
    dot_general x2 -> x0, matrix products: 25.3 us -> none  [the longest x1 18.5 us: local(): jnp.dot(hidden, down_weight, preferred_element_type=jnp.float32)]
    reduce_sum x3 -> x0, other arithmetic: 5.26 us -> none  [the longest x1 5.08 us: local(): jnp.sum(arrived.reshape(members, capacity, features), axis=0, dtype=jnp.f...]
    select_n x3 -> x0, other arithmetic: 4.01 us -> none  [the longest x1 3.99 us: local(): jnp.where(in_use[:, :, None], taken, jnp.zeros_like(taken))]
  transfers between devices with their start and end apart: 1 -> 0, of which waited for: 1 -> 0; matrix products, arithmetic and copies ran while one was open for 1% -> 0% of each run, Pallas kernels for 0% -> 0%
where the time goes in v1:
time: 102 us; the launch traced here: 101 us
  Pallas kernels  75.1 us (74%)
  local copies, waits for them, and re-layouts  26.4 us (26%)
    pallas_call x1, Pallas kernels, local(): pl.pallas_call(kernel, out_shape=jax.ShapeDtypeStruct((capacity, features...  75.1 us
    unnamed x3, local copies, waits for them, and re-layouts  26.4 us

profile of v1, /device:TPU:1, one launch (start us, length us, event | category | flops | bytes accessed | tf_op | source)
XLA Modules:
  0.0 101.5 jit_solution(8071802574684738389)
XLA Ops:
  0.0 12.4 %copy.6.wg_hbm = bf16[7168,576]{1,0:T(8,128)(2,1)} copy(bf16[7168,576]{0,1:T(8,128)(2,1)} %param.7) | data formatting | bytes 16515072 | tf_op args[2]
  12.4 12.4 %copy.7.wu_hbm = bf16[7168,576]{1,0:T(8,128)(2,1)} copy(bf16[7168,576]{0,1:T(8,128)(2,1)} %param.8) | data formatting | bytes 16515072 | tf_op args[3]
  24.8 75.1 %ffn.1 = bf16[16,7168]{1,0:T(8,128)(2,1)} custom-call(bf16[16,7168]{1,0:T(8,128)(2,1)} %req.1, s32[32]{0:T(128)} %counts.1, bf16[7168,576]{1,0:T(8,128)(2,1)} %copy.6.wg_hbm, bf16[7168,576]{1,0:T(8,128)(2,1)} %copy.7.wu_hbm, bf16[576,7168]{1,0:T(8,128)(2,1)} %wd_hbm.1), custom_call_target="tpu_custom_call" | custom-call | flops 6341787648 | bytes 24772608 | tf_op jit(solution)/shard_map/ffn/pallas_call | solution.py:395
  99.9 1.6 %copy.9 = bf16[16,7168]{1,0:T(8,128)(2,1)} copy(bf16[16,7168]{1,0:T(8,128)(2,1)} %ffn.1) | data formatting | bytes 458752

commit v2 on v1

--- a/solution.py
+++ b/solution.py
@@ -25,8 +25,8 @@
 
 
 def kernel(
-    req, counts, wg_hbm, wu_hbm, wd_hbm, out,
-    wg, wu, wd, spread, spread2, pkt, rows_in, inbox, grid, gate, up, hidden,
+    req, counts, wgt_hbm, wut_hbm, wd_hbm, out,
+    wgu, wd, spread, spread2, pkt, rows_in, inbox, grid, acc, hidden,
     pout, pin, chip_sum, big_in, quad_sum, small_in, final, rows_out, pkt_back, inbox_back, offs,
     w_sem, a_send, a_recv, g_send, g_recv, r_send, r_recv, b_send, b_recv,
 ):
@@ -36,6 +36,10 @@
     rp = inbox.shape[1]
     widths = stream_widths(half)
     starts = [sum(widths[:s]) for s in range(4)]
+    order = (0, 2, 1, 3)
+    ff = wd.shape[0]
+    main = ff // LANES * LANES
+    tail = ff - main
 
     me = lax.axis_index("tensor")
     core = lax.rem(me, 2)
@@ -58,16 +62,24 @@
         )
 
     loads = {}
+    pieces = (
+        (wgt_hbm, 0, main, 0),
+        (wut_hbm, 0, main, main),
+        (wgt_hbm, main, tail, 2 * main),
+        (wut_hbm, main, tail, 2 * main + tail),
+    )
     for turn, c in enumerate((core, other)):
-        for s in range(4):
-            rows = pl.ds(pl.multiple_of(c * half + starts[s], LANES), widths[s])
-            pair = []
-            for n, (src, dst) in enumerate(((wg_hbm, wg), (wu_hbm, wu))):
-                copy = pltpu.make_async_copy(src.at[rows], dst.at[rows], w_sem.at[turn * 8 + s * 2 + n])
+        for s in order:
+            col = pl.ds(pl.multiple_of(c * half + starts[s], LANES), widths[s])
+            loads[turn, s] = []
+            for n, (src, at, size, to) in enumerate(pieces):
+                copy = pltpu.make_async_copy(
+                    src.at[pl.ds(at, size), col], wgu.at[pl.ds(to, size), col],
+                    w_sem.at[turn * 16 + s * 4 + n],
+                )
                 copy.start()
-                pair.append(copy)
-            loads[turn, s] = pair
-    wd_load = pltpu.make_async_copy(wd_hbm, wd, w_sem.at[16])
+                loads[turn, s].append(copy)
+    wd_load = pltpu.make_async_copy(wd_hbm, wd, w_sem.at[32])
     wd_load.start()
 
     total = jnp.int32(0)
@@ -129,6 +141,7 @@
     @pl.loop(1, DEVICES)
     def _(s):
         dispatched(s).wait_recv()
+        dispatch(s).wait_send()
 
     for k in range(ROWS // CHIPS):
         spread2[k * rp : (k + 1) * rp, :] = inbox[owners[k]].astype(jnp.float32)
@@ -177,7 +190,6 @@
         ref = quad_of(grid.at[core], s, big)
         gather[s, n] = send(ref, ref, g_send, g_recv, s * 10 + n, target)
 
-    order = (0, 2, 1, 3)
     for s in order:
         small, big = positions[s]
         gather_block(s, 0, small, on_small(s, forward[s]))
@@ -204,14 +216,15 @@
     def contract(c, turn, s):
         for copy in loads[turn, s]:
             copy.wait()
-        rows = pl.ds(pl.multiple_of(c * half + starts[s], LANES), widths[s])
+        col = pl.ds(pl.multiple_of(c * half + starts[s], LANES), widths[s])
         lhs = grid[c, :, :, :, starts[s] : starts[s] + widths[s]].reshape(ROWS, widths[s])
-        for acc, weight in ((gate, wg), (up, wu)):
-            product = jnp.dot(lhs, weight[rows, :], preferred_element_type=jnp.float32)
-            if first[0]:
-                acc[...] = product
-            else:
-                acc[...] += product
+        product = lax.dot_general(
+            lhs, wgu[:, col], (((1,), (1,)), ((), ())), preferred_element_type=jnp.float32
+        )
+        if first[0]:
+            acc[...] = product
+        else:
+            acc[...] += product
         first[0] = False
 
     for s in order:
@@ -226,8 +239,14 @@
             gather[s, n].wait_recv()
         contract(other, 1, s)
 
-    value = gate[...]
-    hidden[...] = (value / (1.0 + jnp.exp(-value)) * up[...]).astype(jnp.bfloat16)
+    def activate(gate, up):
+        return (gate / (1.0 + jnp.exp(-gate)) * up).astype(jnp.bfloat16)
+
+    if main:
+        hidden[:, :main] = activate(acc[:, :main], acc[:, main : 2 * main])
+    if tail:
+        ends_of = acc[:, 2 * main :]
+        hidden[:, main:] = activate(ends_of[:, :tail], ends_of[:, tail:])
     wd_load.wait()
 
     scatter = {}
@@ -356,10 +375,6 @@
     @pl.loop(1, DEVICES)
     def _(s):
         send_back(s).start()
-
-    @pl.loop(1, DEVICES)
-    def _(s):
-        dispatch(s).wait_send()
 
     for copy in list(gather.values()) + list(scatter.values()):
         copy.wait_send()
@@ -404,8 +419,7 @@
         ],
         out_specs=pl.BlockSpec(memory_space=pltpu.VMEM),
         scratch_shapes=[
-            pltpu.VMEM((features, ff), bf16),
-            pltpu.VMEM((features, ff), bf16),
+            pltpu.VMEM((2 * ff, features), bf16),
             pltpu.VMEM((ff, features), bf16),
             pltpu.VMEM((CAP * 2 * rp, LANES), f32),
             pltpu.VMEM((CAP * rp, LANES), f32),
@@ -413,8 +427,7 @@
             pltpu.VMEM((CAP, 2, rp, LANES), bf16),
             pltpu.VMEM((DEVICES, rp, LANES), bf16),
             pltpu.VMEM((2, SIDE, SIDE, CAP, half), bf16),
-            pltpu.VMEM((ROWS, ff), f32),
-            pltpu.VMEM((ROWS, ff), f32),
+            pltpu.VMEM((ROWS, 2 * ff), f32),
             pltpu.VMEM((ROWS, ff), bf16),
             pltpu.VMEM((SIDE, SIDE, CAP, half), bf16),
             pltpu.VMEM((SIDE, SIDE, CAP, half), bf16),
@@ -427,7 +440,7 @@
             pltpu.VMEM((DEVICES, rp, LANES), bf16),
             pltpu.VMEM((DEVICES, rp, LANES), bf16),
             pltpu.SMEM((DEVICES,), jnp.int32),
-            dma((17,)),
+            dma((33,)),
             dma((DEVICES,)),
             dma((DEVICES,)),
             dma((40,)),
@@ -444,7 +457,7 @@
             flops=6 * ROWS * features * ff, bytes_accessed=6 * features * ff, transcendentals=ROWS * ff
         ),
         name="ffn",
-    )(requests, counts, gate_weight, up_weight, down_weight)
+    )(requests, counts, gate_weight.T, up_weight.T, down_weight)
 
 
 def solution(mesh):

time: 102 us -> 77.7 us (0.76)
  local copies, waits for them, and re-layouts: 26.4 us -> 1.64 us
    unnamed x3 -> x1, local copies, waits for them, and re-layouts: 26.4 us -> 1.64 us
where the time goes in v2:
time: 77.7 us; the launch traced here: 77.5 us
  Pallas kernels  75.9 us (98%)
  local copies, waits for them, and re-layouts  1.64 us (2%)
    pallas_call x1, Pallas kernels, local(): pl.pallas_call(kernel, out_shape=jax.ShapeDtypeStruct((capacity, features...  75.9 us
    unnamed x1, local copies, waits for them, and re-layouts  1.64 us

profile of v2, /device:TPU:1, one launch (start us, length us, event | category | flops | bytes accessed | tf_op | source)
XLA Modules:
  0.0 77.5 jit_solution(2337252408351413974)
XLA Ops:
  0.0 75.9 %ffn.1 = bf16[16,7168]{1,0:T(8,128)(2,1)} custom-call(bf16[16,7168]{1,0:T(8,128)(2,1)} %req.1, s32[32]{0:T(128)} %counts.1, bf16[576,7168]{1,0:T(8,128)(2,1)} %bitcast.2, bf16[576,7168]{1,0:T(8,128)(2,1)} %bitcast.3, bf16[576,7168]{1,0:T(8,128)(2,1)} %wd_hbm.1), custom_call_target="tpu_custom_call" | custom-call | flops 6341787648 | bytes 24772608 | tf_op jit(solution)/shard_map/ffn/pallas_call | solution.py:410
  75.9 1.6 %copy.7 = bf16[16,7168]{1,0:T(8,128)(2,1)} copy(bf16[16,7168]{1,0:T(8,128)(2,1)} %ffn.1) | data formatting | bytes 458752

commit v3 on v2

v3 whole, which is shorter than its diff:
```python
import functools

import jax
import jax.numpy as jnp
from jax import lax
from jax.experimental import pallas as pl
from jax.experimental.pallas import tpu as pltpu
from jax.sharding import PartitionSpec as P

SIDE = 4
CHIPS = SIDE * SIDE
DEVICES = 2 * CHIPS
CAP = 16
ROWS = 256
LANES = 128
MESH = pl.DeviceIdType.MESH


def column_pieces(half):
    tile = 256 if half % 512 == 0 and half >= 1024 else 128
    per_order = half // tile // 2
    pieces = []
    for n in range((per_order + 1) // 2):
        for turned in range(2):
            at = (turned * per_order + 2 * n) * tile
            pieces.append((at, min(2, per_order - 2 * n) * tile, turned, n % 2))
    return pieces


def kernel(
    req, counts, wgt_hbm, wut_hbm, wd_hbm, out,
    wgu, wd, spread, spread2, pkt, rows_in, inbox, grid, acc, hidden,
    pout, pin, chip_sum, big_in, quad_sum, small_in, final, rows_out, pkt_back, inbox_back, offs,
    w_sem, a_send, a_recv, g_send, g_recv, r_send, r_recv, b_send, b_recv,
):
    features = req.shape[1]
    half = features // 2
    hb = half // LANES
    rp = inbox.shape[1]
    pieces = column_pieces(half)
    order = range(len(pieces))
    ff = wd.shape[0]
    main = ff // LANES * LANES
    tail = ff - main

    me = lax.axis_index("tensor")
    core = lax.rem(me, 2)
    other = 1 - core
    chip = me // 2
    x = chip // SIDE
    z = lax.rem(chip, SIDE)

    def device(xx, zz, cc):
        return {"tensor": (xx * SIDE + zz) * 2 + cc}

    sibling = device(x, z, other)

    hops = (0, 1, 2, 1)
    others = sorted(
        ((dx, dz, dc) for dx in range(SIDE) for dz in range(SIDE) for dc in range(2) if dx or dz or dc),
        key=lambda o: -hops[o[0]] - hops[o[1]],
    )

    def at_offset(o, sign):
        xx = lax.rem(x + sign * o[0] + SIDE, SIDE)
        zz = lax.rem(z + sign * o[1] + SIDE, SIDE)
        return xx * SIDE + zz, lax.rem(core + o[2], 2)

    def exchange(source, box, sends, recvs):
        copies = []
        for n, o in enumerate(others):
            to_chip, to_core = at_offset(o, 1)
            copy = pltpu.make_async_remote_copy(
                src_ref=source(to_chip, to_core), dst_ref=box.at[me],
                send_sem=sends.at[n], recv_sem=recvs.at[me],
                device_id={"tensor": 2 * to_chip + to_core}, device_id_type=MESH,
            )
            copy.start()
            copies.append(copy)
        return copies

    def arrived(box, sends, recvs):
        for n, o in enumerate(others):
            from_chip, from_core = at_offset(o, -1)
            origin = 2 * from_chip + from_core
            pltpu.make_async_remote_copy(
                src_ref=box.at[me], dst_ref=box.at[origin],
                send_sem=sends.at[n], recv_sem=recvs.at[origin],
                device_id={"tensor": origin}, device_id_type=MESH,
            ).wait_recv()

    barrier = pltpu.get_barrier_semaphore()

    @pl.loop(1, DEVICES)
    def _(s):
        pl.semaphore_signal(
            barrier, inc=1, device_id={"tensor": lax.rem(me + s, DEVICES)}, device_id_type=MESH
        )

    loads = []
    for n, (src, at, size, to) in enumerate((
        (wgt_hbm, 0, main, 0),
        (wut_hbm, 0, main, main),
        (wgt_hbm, main, tail, 2 * main),
        (wut_hbm, main, tail, 2 * main + tail),
    )):
        if size:
            loads.append(
                pltpu.make_async_copy(src.at[pl.ds(at, size)], wgu.at[pl.ds(to, size)], w_sem.at[n])
            )
            loads[-1].start()
    wd_load = pltpu.make_async_copy(wd_hbm, wd, w_sem.at[4])
    wd_load.start()

    total = jnp.int32(0)
    ends = []
    for i in range(DEVICES):
        offs[i] = total
        total = total + counts[i]
        ends.append(total)
    my_off = offs[me]
    my_count = counts[me]

    spread[...] = jnp.zeros_like(spread)
    for h in range(2):
        for m in range(hb):
            block = req[:, (h * hb + m) * LANES : (h * hb + m + 1) * LANES]
            spread[pl.ds(h * rp + m, CAP, stride=2 * rp), :] = block.astype(jnp.float32)

    def row_for(p, off):
        return lax.rem(p - off + ROWS, CAP)

    for j in range(CAP):
        for h in range(2):
            at = (2 * j + h) * rp
            rows_in[j, h] = spread[at : at + rp, :].astype(jnp.bfloat16)
    for p in range(CHIPS):
        pkt[p] = rows_in[row_for(p, my_off)]
    inbox[me] = pkt[chip, core]

    pl.semaphore_wait(barrier, DEVICES - 1)

    dispatched = exchange(lambda p, c: pkt.at[p, c], inbox, a_send, a_recv)

    owners = []
    for k in range(ROWS // CHIPS):
        rank = chip + CHIPS * k
        owner = jnp.int32(0)
        for end in ends[:-1]:
            owner = owner + (end <= rank).astype(jnp.int32)
        owners.append(owner)

    arrived(inbox, a_send, a_recv)

    for k in range(ROWS // CHIPS):
        spread2[k * rp : (k + 1) * rp, :] = inbox[owners[k]].astype(jnp.float32)
    for m in range(hb):
        block = spread2[pl.ds(m, CAP, stride=rp), :].astype(jnp.bfloat16)
        grid[core, x, z, :, m * LANES : (m + 1) * LANES] = block

    def cols(s):
        return pl.ds(pieces[s][0], pieces[s][1])

    def turned(s):
        return pieces[s][2]

    def quad_of(buf, s, big):
        return buf.at[big, :, :, cols(s)] if turned(s) else buf.at[:, big, :, cols(s)]

    positions = [(z, x) if turned(s) else (x, z) for s in order]
    forward = [(1 - 2 * pieces[s][3]) * (1 - 2 * core) for s in order]

    def shift(pos, by):
        return lax.rem(pos + by + 2 * SIDE, SIDE)

    def on_small(s, by):
        return device(x, shift(z, by), core) if turned(s) else device(shift(x, by), z, core)

    def on_big(s, by):
        return device(shift(x, by), z, core) if turned(s) else device(x, shift(z, by), core)

    def send(src, dst, sends, recvs, index, target):
        copy = pltpu.make_async_remote_copy(
            src_ref=src, dst_ref=dst, send_sem=sends.at[index], recv_sem=recvs.at[index],
            device_id=target, device_id_type=MESH,
        )
        copy.start()
        return copy

    gather = {}

    def gather_quad(s, n, big, target):
        ref = quad_of(grid.at[core], s, big)
        gather[s, n] = send(ref, ref, g_send, g_recv, s * 10 + n, target)

    for s in order:
        ref = grid.at[core, x, z, :, cols(s)]
        for by in range(1, SIDE):
            gather[s, by - 1] = send(ref, ref, g_send, g_recv, s * 10 + by - 1, on_small(s, by))
    for s in order:
        big = positions[s][1]
        for n in range(3):
            gather[s, n].wait_recv()
        gather_quad(s, 3, big, on_big(s, forward[s]))
        gather_quad(s, 4, big, on_big(s, -forward[s]))
        gather_quad(s, 6, big, sibling)
    for s in order:
        behind = shift(positions[s][1], -forward[s])
        gather[s, 3].wait_recv()
        gather_quad(s, 5, behind, on_big(s, forward[s]))
        gather_quad(s, 7, behind, sibling)

    for copy in loads:
        copy.wait()

    def contract(c, s):
        at, width = pieces[s][:2]
        col = pl.ds(pl.multiple_of(c * half + at, LANES), width)
        lhs = grid[c, :, :, :, at : at + width].reshape(ROWS, width)
        return lax.dot_general(
            lhs, wgu[:, col], (((1,), (1,)), ((), ())), preferred_element_type=jnp.float32
        )

    def contract_sibling(s):
        for n in (6, 7, 8, 9):
            gather[s, n].wait_recv()
        acc[...] += contract(other, s)

    for s in order:
        big = positions[s][1]
        gather[s, 4].wait_recv()
        gather_quad(s, 8, shift(big, forward[s]), sibling)
        gather[s, 5].wait_recv()
        gather_quad(s, 9, shift(big, 2), sibling)
        if s == 0:
            acc[...] = contract(core, s)
        else:
            acc[...] += contract(core, s)
            contract_sibling(s - 1)
    contract_sibling(len(pieces) - 1)

    def activate(gate, up):
        return (gate / (1.0 + jnp.exp(-gate)) * up).astype(jnp.bfloat16)

    if main:
        hidden[:, :main] = activate(acc[:, :main], acc[:, main : 2 * main])
    if tail:
        ends_of = acc[:, 2 * main :]
        hidden[:, main:] = activate(ends_of[:, :tail], ends_of[:, tail:])
    wd_load.wait()

    scatter = {}

    def partial_cols(c, s):
        at, width = pieces[s][:2]
        col = pl.ds(pl.multiple_of(c * half + at, LANES), width)
        product = jnp.dot(hidden[...], wd[:, col], preferred_element_type=jnp.float32)
        return product.reshape(SIDE, SIDE, CAP, width)

    def scatter_send(s, n, src, dst, target):
        scatter[s, n] = send(src, dst, r_send, r_recv, s * 7 + n, target)

    def to_sibling(s):
        c = cols(s)
        pout[:, :, :, c] = partial_cols(other, s).astype(jnp.bfloat16)
        scatter_send(s, 0, pout.at[:, :, :, c], pin.at[:, :, :, c], sibling)

    def add_cores(s):
        c = cols(s)
        big, d = positions[s][1], forward[s]
        mine = partial_cols(core, s)
        scatter[s, 0].wait_recv()
        chip_sum[:, :, :, c] = (mine + pin[:, :, :, c].astype(jnp.float32)).astype(jnp.bfloat16)
        scatter_send(s, 1, quad_of(chip_sum, s, shift(big, 2)), big_in.at[0, :, :, c], on_big(s, d))
        scatter_send(s, 2, quad_of(chip_sum, s, shift(big, -d)), big_in.at[1, :, :, c], on_big(s, -d))

    def quad_load(s, big):
        c = cols(s)
        return (chip_sum[big, :, :, c] if turned(s) else chip_sum[:, big, :, c]).astype(jnp.float32)

    def relay_quad(s):
        c = cols(s)
        big, d = positions[s][1], forward[s]
        scatter[s, 1].wait_recv()
        big_in[0, :, :, c] = (
            quad_load(s, shift(big, d)) + big_in[0, :, :, c].astype(jnp.float32)
        ).astype(jnp.bfloat16)
        scatter_send(s, 3, big_in.at[0, :, :, c], big_in.at[2, :, :, c], on_big(s, d))

    def start_small(s):
        c = cols(s)
        small, big = positions[s]
        scatter[s, 2].wait_recv()
        scatter[s, 3].wait_recv()
        quad_sum[:, :, c] = (
            quad_load(s, big)
            + big_in[1, :, :, c].astype(jnp.float32)
            + big_in[2, :, :, c].astype(jnp.float32)
        ).astype(jnp.bfloat16)
        for by in range(1, SIDE):
            scatter_send(
                s, 3 + by, quad_sum.at[shift(small, by), :, c], small_in.at[by - 1, :, c], on_small(s, by)
            )

    def finish(s):
        c = cols(s)
        small = positions[s][0]
        value = quad_sum[small, :, c].astype(jnp.float32)
        for n in range(SIDE - 1):
            scatter[s, 4 + n].wait_recv()
            value = value + small_in[n, :, c].astype(jnp.float32)
        final[:, c] = value

    to_sibling(0)
    for s in order:
        if s + 1 < len(pieces):
            to_sibling(s + 1)
        add_cores(s)
    for stage in (relay_quad, start_small, finish):
        for s in order:
            stage(s)

    for m in range(hb):
        spread2[pl.ds(m, CAP, stride=rp), :] = final[:, m * LANES : (m + 1) * LANES]
    for k in range(ROWS // CHIPS):
        rows_out[k] = spread2[k * rp : (k + 1) * rp, :].astype(jnp.bfloat16)
    for i in range(DEVICES):
        rank = offs[i] + row_for(chip, offs[i])
        pkt_back[i] = rows_out[jnp.minimum(rank // CHIPS, ROWS // CHIPS - 1)]
    inbox_back[me] = pkt_back[me]

    returned = exchange(lambda p, c: pkt_back.at[2 * p + c], inbox_back, b_send, b_recv)

    for copy in dispatched + list(gather.values()) + list(scatter.values()):
        copy.wait_send()
    arrived(inbox_back, b_send, b_recv)

    for j in range(CAP):
        p = lax.rem(my_off + j, CHIPS)
        for h in range(2):
            row = inbox_back[2 * p + h].astype(jnp.float32)
            row = jnp.where(j < my_count, row, jnp.zeros_like(row))
            spread[(2 * j + h) * rp : (2 * j + h + 1) * rp, :] = row
    for h in range(2):
        for m in range(hb):
            block = spread[pl.ds(h * rp + m, CAP, stride=2 * rp), :]
            at = (h * hb + m) * LANES
            out[:, at : at + LANES] = block.astype(jnp.bfloat16)
    for copy in returned:
        copy.wait_send()


def local(requests, counts, gate_weight, up_weight, down_weight):
    capacity, features = requests.shape
    ff = gate_weight.shape[1]
    half = features // 2
    n_pieces = len(column_pieces(half))
    rp = -(-(half // LANES) // 16) * 16
    bf16, f32 = jnp.bfloat16, jnp.float32
    dma = pltpu.SemaphoreType.DMA
    return pl.pallas_call(
        kernel,
        out_shape=jax.ShapeDtypeStruct((capacity, features), bf16),
        in_specs=[
            pl.BlockSpec(memory_space=pltpu.VMEM),
            pl.BlockSpec(memory_space=pltpu.SMEM),
            pl.BlockSpec(memory_space=pl.ANY),
            pl.BlockSpec(memory_space=pl.ANY),
            pl.BlockSpec(memory_space=pl.ANY),
        ],
        out_specs=pl.BlockSpec(memory_space=pltpu.VMEM),
        scratch_shapes=[
            pltpu.VMEM((2 * ff, features), bf16),
            pltpu.VMEM((ff, features), bf16),
            pltpu.VMEM((CAP * 2 * rp, LANES), f32),
            pltpu.VMEM((CAP * rp, LANES), f32),
            pltpu.VMEM((CHIPS, 2, rp, LANES), bf16),
            pltpu.VMEM((CAP, 2, rp, LANES), bf16),
            pltpu.VMEM((DEVICES, rp, LANES), bf16),
            pltpu.VMEM((2, SIDE, SIDE, CAP, half), bf16),
            pltpu.VMEM((ROWS, 2 * ff), f32),
            pltpu.VMEM((ROWS, ff), bf16),
            pltpu.VMEM((SIDE, SIDE, CAP, half), bf16),
            pltpu.VMEM((SIDE, SIDE, CAP, half), bf16),
            pltpu.VMEM((SIDE, SIDE, CAP, half), bf16),
            pltpu.VMEM((3, SIDE, CAP, half), bf16),
            pltpu.VMEM((SIDE, CAP, half), bf16),
            pltpu.VMEM((3, CAP, half), bf16),
            pltpu.VMEM((CAP, half), f32),
            pltpu.VMEM((ROWS // CHIPS, rp, LANES), bf16),
            pltpu.VMEM((DEVICES, rp, LANES), bf16),
            pltpu.VMEM((DEVICES, rp, LANES), bf16),
            pltpu.SMEM((DEVICES,), jnp.int32),
            dma((5,)),
            dma((DEVICES,)),
            dma((DEVICES,)),
            dma((n_pieces * 10,)),
            dma((n_pieces * 10,)),
            dma((n_pieces * 7,)),
            dma((n_pieces * 7,)),
            dma((DEVICES,)),
            dma((DEVICES,)),
        ],
        compiler_params=pltpu.CompilerParams(
            collective_id=0, has_side_effects=True, vmem_limit_bytes=58 * 2**20
        ),
        cost_estimate=pl.CostEstimate(
            flops=6 * ROWS * features * ff, bytes_accessed=6 * features * ff, transcendentals=ROWS * ff
        ),
        name="ffn",
    )(requests, counts, gate_weight.T, up_weight.T, down_weight)


def solution(mesh):
    return jax.shard_map(
        local,
        mesh=mesh,
        in_specs=(
            P(("group", "tensor"), None),
            P("group"),
            P(None, "tensor"),
            P(None, "tensor"),
            P("tensor", None),
        ),
        out_specs=P(("group", "tensor"), None),
        check_vma=False,
    )
```

time: 77.7 us -> 65 us (0.84)
  Pallas kernels: 75.9 us -> 63.2 us
    pallas_call x1, Pallas kernels: 75.9 us -> 63.2 us  [local(): pl.pallas_call(kernel, out_shape=jax.ShapeDtypeStruct((capacity, features...]
where the time goes in v3:
time: 65 us; the launch traced here: 64.9 us
  Pallas kernels  63.2 us (97%)
  local copies, waits for them, and re-layouts  1.64 us (3%)
    pallas_call x1, Pallas kernels, local(): pl.pallas_call(kernel, out_shape=jax.ShapeDtypeStruct((capacity, features...  63.2 us
    unnamed x1, local copies, waits for them, and re-layouts  1.64 us

profile of v3, /device:TPU:1, one launch (start us, length us, event | category | flops | bytes accessed | tf_op | source)
XLA Modules:
  0.0 64.9 jit_solution(18267398022227518661)
XLA Ops:
  0.0 63.2 %ffn.1 = bf16[16,7168]{1,0:T(8,128)(2,1)} custom-call(bf16[16,7168]{1,0:T(8,128)(2,1)} %req.1, s32[32]{0:T(128)} %counts.1, bf16[576,7168]{1,0:T(8,128)(2,1)} %bitcast.2, bf16[576,7168]{1,0:T(8,128)(2,1)} %bitcast.3, bf16[576,7168]{1,0:T(8,128)(2,1)} %wd_hbm.1), custom_call_target="tpu_custom_call" | custom-call | flops 6341787648 | bytes 24772608 | tf_op jit(solution)/shard_map/ffn/pallas_call | solution.py:361
  63.2 1.6 %copy.7 = bf16[16,7168]{1,0:T(8,128)(2,1)} copy(bf16[16,7168]{1,0:T(8,128)(2,1)} %ffn.1) | data formatting | bytes 458752

commit v4 on v3

--- a/solution.py
+++ b/solution.py
@@ -28,10 +28,10 @@
 
 
 def kernel(
-    req, counts, wgt_hbm, wut_hbm, wd_hbm, out,
-    wgu, wd, spread, spread2, pkt, rows_in, inbox, grid, acc, hidden,
-    pout, pin, chip_sum, big_in, quad_sum, small_in, final, rows_out, pkt_back, inbox_back, offs,
-    w_sem, a_send, a_recv, g_send, g_recv, r_send, r_recv, b_send, b_recv,
+    req_hbm, counts, wgt_hbm, wut_hbm, wd_hbm, out,
+    req, wgu, wd, spread, spread2, pkt, rows_in, inbox, grid, acc, hidden,
+    chip_sum, big_in, quad_sum, small_in, final, rows_out, pkt_back, inbox_back, offs,
+    w_sem, s_send, s_recv, a_send, a_recv, g_send, g_recv, r_send, r_recv, b_send, b_recv,
 ):
     features = req.shape[1]
     half = features // 2
@@ -39,7 +39,7 @@
     rp = inbox.shape[1]
     pieces = column_pieces(half)
     order = range(len(pieces))
-    ff = wd.shape[0]
+    ff = wd.shape[1]
     main = ff // LANES * LANES
     tail = ff - main
 
@@ -89,6 +89,9 @@
                 device_id={"tensor": origin}, device_id_type=MESH,
             ).wait_recv()
 
+    req_load = pltpu.make_async_copy(req_hbm, req, w_sem.at[5])
+    req_load.start()
+
     barrier = pltpu.get_barrier_semaphore()
 
     @pl.loop(1, DEVICES)
@@ -109,7 +112,9 @@
                 pltpu.make_async_copy(src.at[pl.ds(at, size)], wgu.at[pl.ds(to, size)], w_sem.at[n])
             )
             loads[-1].start()
-    wd_load = pltpu.make_async_copy(wd_hbm, wd, w_sem.at[4])
+    wd_load = pltpu.make_async_copy(
+        wd_hbm.at[:, pl.ds(pl.multiple_of(core * half, LANES), half)], wd.at[0], w_sem.at[4]
+    )
     wd_load.start()
 
     total = jnp.int32(0)
@@ -122,6 +127,7 @@
     my_count = counts[me]
 
     spread[...] = jnp.zeros_like(spread)
+    req_load.wait()
     for h in range(2):
         for m in range(hb):
             block = req[:, (h * hb + m) * LANES : (h * hb + m + 1) * LANES]
@@ -140,7 +146,13 @@
 
     pl.semaphore_wait(barrier, DEVICES - 1)
 
+    wd_share = pltpu.make_async_remote_copy(
+        src_ref=wd_hbm.at[:, pl.ds(pl.multiple_of(other * half, LANES), half)], dst_ref=wd.at[1],
+        send_sem=s_send.at[0], recv_sem=s_recv.at[0], device_id=sibling, device_id_type=MESH,
+    )
     dispatched = exchange(lambda p, c: pkt.at[p, c], inbox, a_send, a_recv)
+
+    wd_share.start()
 
     owners = []
     for k in range(ROWS // CHIPS):
@@ -221,56 +233,64 @@
             lhs, wgu[:, col], (((1,), (1,)), ((), ())), preferred_element_type=jnp.float32
         )
 
-    def contract_sibling(s):
-        for n in (6, 7, 8, 9):
-            gather[s, n].wait_recv()
-        acc[...] += contract(other, s)
-
-    for s in order:
+    def arrive(s):
         big = positions[s][1]
         gather[s, 4].wait_recv()
         gather_quad(s, 8, shift(big, forward[s]), sibling)
         gather[s, 5].wait_recv()
         gather_quad(s, 9, shift(big, 2), sibling)
-        if s == 0:
-            acc[...] = contract(core, s)
-        else:
-            acc[...] += contract(core, s)
-            contract_sibling(s - 1)
-    contract_sibling(len(pieces) - 1)
+
+    def from_sibling(s):
+        for n in (6, 7, 8, 9):
+            gather[s, n].wait_recv()
+
+    first, second = order[: len(pieces) // 2], order[len(pieces) // 2 :]
+    for s in first:
+        arrive(s)
+    acc[...] = sum(contract(core, s) for s in first)
+    for s in second:
+        arrive(s)
+    for s in first:
+        from_sibling(s)
+    acc[...] += sum([contract(core, s) for s in second] + [contract(other, s) for s in first])
+    for s in second:
+        from_sibling(s)
+    acc[...] += sum(contract(other, s) for s in second)
 
     def activate(gate, up):
         return (gate / (1.0 + jnp.exp(-gate)) * up).astype(jnp.bfloat16)
 
     if main:
-        hidden[:, :main] = activate(acc[:, :main], acc[:, main : 2 * main])
+        hidden[0, :, :main] = activate(acc[:, :main], acc[:, main : 2 * main])
     if tail:
         ends_of = acc[:, 2 * main :]
-        hidden[:, main:] = activate(ends_of[:, :tail], ends_of[:, tail:])
+        hidden[0, :, main:] = activate(ends_of[:, :tail], ends_of[:, tail:])
+
+    hidden_share = pltpu.make_async_remote_copy(
+        src_ref=hidden.at[0], dst_ref=hidden.at[1],
+        send_sem=s_send.at[1], recv_sem=s_recv.at[1], device_id=sibling, device_id_type=MESH,
+    )
+    hidden_share.start()
     wd_load.wait()
+    wd_share.wait_recv()
+    hidden_share.wait_recv()
 
     scatter = {}
 
-    def partial_cols(c, s):
-        at, width = pieces[s][:2]
-        col = pl.ds(pl.multiple_of(c * half + at, LANES), width)
-        product = jnp.dot(hidden[...], wd[:, col], preferred_element_type=jnp.float32)
-        return product.reshape(SIDE, SIDE, CAP, width)
+    def product(n, s):
+        return jnp.dot(hidden[n], wd[n, :, cols(s)], preferred_element_type=jnp.float32)
 
     def scatter_send(s, n, src, dst, target):
         scatter[s, n] = send(src, dst, r_send, r_recv, s * 7 + n, target)
 
-    def to_sibling(s):
-        c = cols(s)
-        pout[:, :, :, c] = partial_cols(other, s).astype(jnp.bfloat16)
-        scatter_send(s, 0, pout.at[:, :, :, c], pin.at[:, :, :, c], sibling)
-
     def add_cores(s):
+        chip_sum[:, :, :, cols(s)] = (
+            (product(0, s) + product(1, s)).astype(jnp.bfloat16).reshape(SIDE, SIDE, CAP, pieces[s][1])
+        )
+
+    def start_big(s):
         c = cols(s)
         big, d = positions[s][1], forward[s]
-        mine = partial_cols(core, s)
-        scatter[s, 0].wait_recv()
-        chip_sum[:, :, :, c] = (mine + pin[:, :, :, c].astype(jnp.float32)).astype(jnp.bfloat16)
         scatter_send(s, 1, quad_of(chip_sum, s, shift(big, 2)), big_in.at[0, :, :, c], on_big(s, d))
         scatter_send(s, 2, quad_of(chip_sum, s, shift(big, -d)), big_in.at[1, :, :, c], on_big(s, -d))
 
@@ -278,47 +298,63 @@
         c = cols(s)
         return (chip_sum[big, :, :, c] if turned(s) else chip_sum[:, big, :, c]).astype(jnp.float32)
 
-    def relay_quad(s):
-        c = cols(s)
-        big, d = positions[s][1], forward[s]
-        scatter[s, 1].wait_recv()
+    def add_relay(s):
+        c = cols(s)
         big_in[0, :, :, c] = (
-            quad_load(s, shift(big, d)) + big_in[0, :, :, c].astype(jnp.float32)
+            quad_load(s, shift(positions[s][1], forward[s])) + big_in[0, :, :, c].astype(jnp.float32)
         ).astype(jnp.bfloat16)
-        scatter_send(s, 3, big_in.at[0, :, :, c], big_in.at[2, :, :, c], on_big(s, d))
-
-    def start_small(s):
-        c = cols(s)
-        small, big = positions[s]
-        scatter[s, 2].wait_recv()
-        scatter[s, 3].wait_recv()
+
+    def relay(s):
+        c = cols(s)
+        scatter_send(s, 3, big_in.at[0, :, :, c], big_in.at[2, :, :, c], on_big(s, forward[s]))
+
+    def add_quads(s):
+        c = cols(s)
         quad_sum[:, :, c] = (
-            quad_load(s, big)
+            quad_load(s, positions[s][1])
             + big_in[1, :, :, c].astype(jnp.float32)
             + big_in[2, :, :, c].astype(jnp.float32)
         ).astype(jnp.bfloat16)
+
+    def start_small(s):
+        c = cols(s)
         for by in range(1, SIDE):
             scatter_send(
-                s, 3 + by, quad_sum.at[shift(small, by), :, c], small_in.at[by - 1, :, c], on_small(s, by)
+                s, 3 + by, quad_sum.at[shift(positions[s][0], by), :, c],
+                small_in.at[by - 1, :, c], on_small(s, by),
             )
 
-    def finish(s):
-        c = cols(s)
-        small = positions[s][0]
-        value = quad_sum[small, :, c].astype(jnp.float32)
+    def add_blocks(s):
+        c = cols(s)
+        value = quad_sum[positions[s][0], :, c].astype(jnp.float32)
         for n in range(SIDE - 1):
-            scatter[s, 4 + n].wait_recv()
             value = value + small_in[n, :, c].astype(jnp.float32)
         final[:, c] = value
 
-    to_sibling(0)
-    for s in order:
-        if s + 1 < len(pieces):
-            to_sibling(s + 1)
-        add_cores(s)
-    for stage in (relay_quad, start_small, finish):
-        for s in order:
-            stage(s)
+    def step(waits, work, sends):
+        for s, n in waits:
+            scatter[s, n].wait_recv()
+        for act, group in work:
+            for s in group:
+                act(s)
+        for act, group in sends:
+            for s in group:
+                act(s)
+
+    def came(group, *ns):
+        return [(s, n) for s in group for n in ns]
+
+    groups = [order[n : n + 2] for n in range(0, len(pieces), 2)]
+    for n, group in enumerate(groups):
+        step([], [(add_cores, group)], [(start_big, group)])
+        if n == 3:
+            step(came(groups[0], 1), [(add_relay, groups[0])], [(relay, groups[0])])
+    for group in groups[1:]:
+        step(came(group, 1), [(add_relay, group)], [(relay, group)])
+    for group in groups:
+        step(came(group, 2, 3), [(add_quads, group)], [(start_small, group)])
+    for group in groups:
+        step(came(group, 4, 5, 6), [(add_blocks, group)], [])
 
     for m in range(hb):
         spread2[pl.ds(m, CAP, stride=rp), :] = final[:, m * LANES : (m + 1) * LANES]
@@ -331,7 +367,7 @@
 
     returned = exchange(lambda p, c: pkt_back.at[2 * p + c], inbox_back, b_send, b_recv)
 
-    for copy in dispatched + list(gather.values()) + list(scatter.values()):
+    for copy in [wd_share, hidden_share] + dispatched + list(gather.values()) + list(scatter.values()):
         copy.wait_send()
     arrived(inbox_back, b_send, b_recv)
 
@@ -362,7 +398,7 @@
         kernel,
         out_shape=jax.ShapeDtypeStruct((capacity, features), bf16),
         in_specs=[
-            pl.BlockSpec(memory_space=pltpu.VMEM),
+            pl.BlockSpec(memory_space=pl.ANY),
             pl.BlockSpec(memory_space=pltpu.SMEM),
             pl.BlockSpec(memory_space=pl.ANY),
             pl.BlockSpec(memory_space=pl.ANY),
@@ -370,8 +406,9 @@
         ],
         out_specs=pl.BlockSpec(memory_space=pltpu.VMEM),
         scratch_shapes=[
+            pltpu.VMEM((capacity, features), bf16),
             pltpu.VMEM((2 * ff, features), bf16),
-            pltpu.VMEM((ff, features), bf16),
+            pltpu.VMEM((2, ff, half), bf16),
             pltpu.VMEM((CAP * 2 * rp, LANES), f32),
             pltpu.VMEM((CAP * rp, LANES), f32),
             pltpu.VMEM((CHIPS, 2, rp, LANES), bf16),
@@ -379,9 +416,7 @@
             pltpu.VMEM((DEVICES, rp, LANES), bf16),
             pltpu.VMEM((2, SIDE, SIDE, CAP, half), bf16),
             pltpu.VMEM((ROWS, 2 * ff), f32),
-            pltpu.VMEM((ROWS, ff), bf16),
-            pltpu.VMEM((SIDE, SIDE, CAP, half), bf16),
-            pltpu.VMEM((SIDE, SIDE, CAP, half), bf16),
+            pltpu.VMEM((2, ROWS, ff), bf16),
             pltpu.VMEM((SIDE, SIDE, CAP, half), bf16),
             pltpu.VMEM((3, SIDE, CAP, half), bf16),
             pltpu.VMEM((SIDE, CAP, half), bf16),
@@ -391,7 +426,9 @@
             pltpu.VMEM((DEVICES, rp, LANES), bf16),
             pltpu.VMEM((DEVICES, rp, LANES), bf16),
             pltpu.SMEM((DEVICES,), jnp.int32),
-            dma((5,)),
+            dma((6,)),
+            dma((2,)),
+            dma((2,)),
             dma((DEVICES,)),
             dma((DEVICES,)),
             dma((n_pieces * 10,)),

time: 65 us -> 63.4 us (0.975)
  Pallas kernels: 63.2 us -> 61.6 us
    pallas_call x1, Pallas kernels: 63.2 us -> 61.6 us  [local(): pl.pallas_call(kernel, out_shape=jax.ShapeDtypeStruct((capacity, features...]
where the time goes in v4:
time: 63.4 us; the launch traced here: 63.2 us
  Pallas kernels  61.6 us (97%)
  local copies, waits for them, and re-layouts  1.64 us (3%)
    pallas_call x1, Pallas kernels, local(): pl.pallas_call(kernel, out_shape=jax.ShapeDtypeStruct((capacity, features...  61.6 us
    unnamed x1, local copies, waits for them, and re-layouts  1.64 us

profile of v4, /device:TPU:1, one launch (start us, length us, event | category | flops | bytes accessed | tf_op | source)
XLA Modules:
  0.0 63.2 jit_solution(14519678225230444775)
XLA Ops:
  0.0 61.6 %ffn.1 = bf16[16,7168]{1,0:T(8,128)(2,1)} custom-call(bf16[16,7168]{1,0:T(8,128)(2,1)} %req_hbm.1, s32[32]{0:T(128)} %counts.1, bf16[576,7168]{1,0:T(8,128)(2,1)} %bitcast.2, bf16[576,7168]{1,0:T(8,128)(2,1)} %bitcast.3, bf16[576,7168]{1,0:T(8,128)(2,1)} %wd_hbm.1), custom_call_target="tpu_custom_call" | custom-call | flops 6341787648 | bytes 24772608 | tf_op jit(solution)/shard_map/ffn/pallas_call | solution.py:397
  61.6 1.6 %copy.7 = bf16[16,7168]{1,0:T(8,128)(2,1)} copy(bf16[16,7168]{1,0:T(8,128)(2,1)} %ffn.1) | data formatting | bytes 458752

commit v5 on v4

--- a/solution.py
+++ b/solution.py
@@ -55,17 +55,6 @@
 
     sibling = device(x, z, other)
 
-    hops = (0, 1, 2, 1)
-    others = sorted(
-        ((dx, dz, dc) for dx in range(SIDE) for dz in range(SIDE) for dc in range(2) if dx or dz or dc),
-        key=lambda o: -hops[o[0]] - hops[o[1]],
-    )
-
-    def at_offset(o, sign):
-        xx = lax.rem(x + sign * o[0] + SIDE, SIDE)
-        zz = lax.rem(z + sign * o[1] + SIDE, SIDE)
-        return xx * SIDE + zz, lax.rem(core + o[2], 2)
-
     def exchange(source, box, sends, recvs):
         copies = []
         for n, o in enumerate(others):
@@ -89,15 +78,26 @@
                 device_id={"tensor": origin}, device_id_type=MESH,
             ).wait_recv()
 
+    hops = (0, 1, 2, 1)
+    others = sorted(
+        ((dx, dz, dc) for dx in range(SIDE) for dz in range(SIDE) for dc in range(2) if dx or dz or dc),
+        key=lambda o: -hops[o[0]] - hops[o[1]],
+    )
+
+    def at_offset(o, sign):
+        xx = lax.rem(x + sign * o[0] + SIDE, SIDE)
+        zz = lax.rem(z + sign * o[1] + SIDE, SIDE)
+        return xx * SIDE + zz, lax.rem(core + o[2], 2)
+
     req_load = pltpu.make_async_copy(req_hbm, req, w_sem.at[5])
     req_load.start()
 
     barrier = pltpu.get_barrier_semaphore()
 
-    @pl.loop(1, DEVICES)
-    def _(s):
+    for o in others:
+        to_chip, to_core = at_offset(o, 1)
         pl.semaphore_signal(
-            barrier, inc=1, device_id={"tensor": lax.rem(me + s, DEVICES)}, device_id_type=MESH
+            barrier, inc=1, device_id={"tensor": 2 * to_chip + to_core}, device_id_type=MESH
         )
 
     loads = []

time: 63.4 us -> 63.2 us (level)
  no operation moved by 1% of the time
where the time goes in v5:
time: 63.2 us; the launch traced here: 63.1 us
  Pallas kernels  61.4 us (97%)
  local copies, waits for them, and re-layouts  1.64 us (3%)
    pallas_call x1, Pallas kernels, local(): pl.pallas_call(kernel, out_shape=jax.ShapeDtypeStruct((capacity, features...  61.4 us
    unnamed x1, local copies, waits for them, and re-layouts  1.64 us

profile of v5, /device:TPU:1, one launch (start us, length us, event | category | flops | bytes accessed | tf_op | source)
XLA Modules:
  0.0 63.1 jit_solution(15512884832570181930)
XLA Ops:
  0.0 61.4 %ffn.1 = bf16[16,7168]{1,0:T(8,128)(2,1)} custom-call(bf16[16,7168]{1,0:T(8,128)(2,1)} %req_hbm.1, s32[32]{0:T(128)} %counts.1, bf16[576,7168]{1,0:T(8,128)(2,1)} %bitcast.2, bf16[576,7168]{1,0:T(8,128)(2,1)} %bitcast.3, bf16[576,7168]{1,0:T(8,128)(2,1)} %wd_hbm.1), custom_call_target="tpu_custom_call" | custom-call | flops 6341787648 | bytes 24772608 | tf_op jit(solution)/shard_map/ffn/pallas_call | solution.py:397
  61.5 1.6 %copy.7 = bf16[16,7168]{1,0:T(8,128)(2,1)} copy(bf16[16,7168]{1,0:T(8,128)(2,1)} %ffn.1) | data formatting | bytes 458752

commit v6 on v5

--- a/solution.py
+++ b/solution.py
@@ -409,8 +409,8 @@
             pltpu.VMEM((capacity, features), bf16),
             pltpu.VMEM((2 * ff, features), bf16),
             pltpu.VMEM((2, ff, half), bf16),
-            pltpu.VMEM((CAP * 2 * rp, LANES), f32),
-            pltpu.VMEM((CAP * rp, LANES), f32),
+            pltpu.VMEM(((CAP + 1) * 2 * rp, LANES), f32),
+            pltpu.VMEM(((CAP + 1) * rp, LANES), f32),
             pltpu.VMEM((CHIPS, 2, rp, LANES), bf16),
             pltpu.VMEM((CAP, 2, rp, LANES), bf16),
             pltpu.VMEM((DEVICES, rp, LANES), bf16),

time: 63.2 us -> 63.2 us (level)
  no operation moved by 1% of the time
where the time goes in v6:
time: 63.2 us; the launch traced here: 63.1 us
  Pallas kernels  61.4 us (97%)
  local copies, waits for them, and re-layouts  1.64 us (3%)
    pallas_call x1, Pallas kernels, local(): pl.pallas_call(kernel, out_shape=jax.ShapeDtypeStruct((capacity, features...  61.4 us
    unnamed x1, local copies, waits for them, and re-layouts  1.64 us

profile of v6, /device:TPU:1, one launch (start us, length us, event | category | flops | bytes accessed | tf_op | source)
XLA Modules:
  0.0 63.1 jit_solution(13917510295509618161)
XLA Ops:
  0.0 61.4 %ffn.1 = bf16[16,7168]{1,0:T(8,128)(2,1)} custom-call(bf16[16,7168]{1,0:T(8,128)(2,1)} %req_hbm.1, s32[32]{0:T(128)} %counts.1, bf16[576,7168]{1,0:T(8,128)(2,1)} %bitcast.2, bf16[576,7168]{1,0:T(8,128)(2,1)} %bitcast.3, bf16[576,7168]{1,0:T(8,128)(2,1)} %wd_hbm.1), custom_call_target="tpu_custom_call" | custom-call | flops 6341787648 | bytes 24772608 | tf_op jit(solution)/shard_map/ffn/pallas_call | solution.py:397
  61.5 1.6 %copy.7 = bf16[16,7168]{1,0:T(8,128)(2,1)} copy(bf16[16,7168]{1,0:T(8,128)(2,1)} %ffn.1) | data formatting | bytes 458752
